TPU v7x, 128 devices: a whole 4x4x4 slice. The times are simulated.
128 devices in a mesh: lat: 8 (over y_lo, x), lon: 16 (over y_hi, z, core).
Axes of the slice: x: 4, y: 4 (y_hi: 2, y_lo: 2; y = y_hi * 2 + y_lo), z: 4, core: 2. Of those that a mesh axis runs over, the one named last changes fastest.
Arguments:
- inputs: float32 [1, 128, 256, 384], P(None, 'lat', 'lon'), may hold values from -6 to 6
- saved: float32 [1, 128, 256, 384], P(None, 'lat', 'lon'), may hold values from -6 to 6
- grad_out: float32 [1, 128, 256, 384], P(None, 'lat', 'lon'), may hold values from -6 to 6
- w_up: float32 [384, 768], replicated, may hold values from -0.3125 to 0.3125
- w_down: float32 [768, 384], replicated, may hold values from -0.21875 to 0.21875
- w_filter: float32 [128, 384, 384], P('lon'), may hold values from -0.3125 to 0.3125
Outputs:
- grad_input: float32 [1, 128, 256, 384], P(None, 'lat', 'lon')
- grad_up: float32 [384, 768], P(None, ('lat', 'lon'))
- grad_down: float32 [768, 384], P(('lat', 'lon'))
- grad_filter: float32 [128, 384, 384], P('lon', 'lat')
All inputs are finite; a program needn't handle non-finite values.
Results may differ from a plain program's by a relative error of at most 0.0003.
Values sent between devices are 32-bit elements; how exact they have to be, the bound alone decides.
A program may use at most 128 MiB of HBM per device.

v0:
```python
import math

import jax
import jax.numpy as jnp
import numpy as np
from jax import lax
from jax.experimental import pallas as pl
from jax.experimental.pallas import tpu as pltpu
from jax.sharding import PartitionSpec as P

NLAT = 128
NLON = 256
MODES = 128
WIDTH = 384
HIDDEN = 768
SAMPLES = 1
NDEV = 128
LON = 16
LAT = 8
POINTS = 256
MESH = pl.DeviceIdType.MESH
F32 = jnp.float32
BF16 = jnp.bfloat16

NN = (((1,), (0,)), ((), ()))
NT = (((1,), (1,)), ((), ()))
TN = (((0,), (0,)), ((), ()))


def legendre_values():
    theta = np.pi * (np.arange(NLAT) + 0.5) / NLAT
    cosines, sines = np.cos(theta), np.sin(theta)
    order = np.arange(MODES, dtype=np.float64)[:, None]
    k = np.arange(1, MODES, dtype=np.float64)
    log_prod = np.concatenate([[0.0], np.cumsum(np.log((2 * k - 1) / (2 * k)))])
    initial = np.exp(
        0.5 * np.log((2 * order + 1) / (4 * np.pi))
        + 0.5 * log_prod[:, None]
        + order * np.log(sines)[None, :]
    )
    previous = np.zeros((MODES, NLAT))
    earlier = np.zeros((MODES, NLAT))
    rows = []
    for degree in range(MODES):
        l = float(degree)
        a = np.sqrt(np.maximum(4 * l * l - 1, 1) / np.maximum(l * l - order * order, 1))
        b = np.sqrt(
            np.maximum((l - 1) ** 2 - order * order, 0) / np.maximum(4 * (l - 1) ** 2 - 1, 1)
        )
        grown = a * (cosines[None, :] * previous - b * earlier)
        current = np.where(order == l, initial, np.where(order < l, grown, 0.0))
        previous, earlier = current, previous
        rows.append(current)
    table = np.stack(rows, axis=1)
    return table * np.sqrt(2 * np.pi * np.pi * sines / NLAT)[None, None, :]


def fourier_values():
    phase = (np.arange(NLON)[:, None] * np.arange(MODES)[None, :]) % NLON
    angle = 2 * np.pi * phase / NLON
    return np.concatenate([np.cos(angle), -np.sin(angle)], axis=1) * np.sqrt(2.0 / NLON)


def halves(table):
    table = np.asarray(table, np.float32)
    high = table.astype(jnp.bfloat16)
    low = (table - high.astype(np.float32)).astype(jnp.bfloat16)
    return high, low


def split(x):
    high = x.astype(BF16)
    return high, (x - high.astype(F32)).astype(BF16)


def dot3(a, b, dims):
    def dot(u, v):
        return lax.dot_general(u, v, dims, preferred_element_type=F32)

    return dot(a[0], b[0]) + (dot(a[0], b[1]) + dot(a[1], b[0]))


def exchange(tiles, lane):
    tiles = list(tiles)
    for bit in (1, 2, 4):
        upper = jnp.bitwise_and(lane, 16 * bit) != 0
        for s in range(8):
            if s & bit:
                continue
            lo, hi = tiles[s], tiles[s | bit]
            tiles[s] = jnp.where(upper, pltpu.roll(hi, 16 * bit, 1), lo)
            tiles[s | bit] = jnp.where(upper, hi, pltpu.roll(lo, 128 - 16 * bit, 1))
    return tiles


def kernel(
    x_hbm, saved_hbm, gout_hbm, up_hbm, down_hbm, filt_hbm, ta_hbm, ts_hbm, fo_hbm,
    gin_out, up_out, gf_out,
    x, saved, gout, up, down, filt, ta, ts, fo,
    send1, recv1, send2, recv2, send3, recv3, send4, recv4,
    act, gpre, field, part, pieces, pair, others, circle, zbuf, wbuf, spec, gfil, gfrecv, sums,
    load_sem, ssem, rsem, psem, osem, gsem, out_sem,
):
    lat = lax.axis_index("lat")
    lon = lax.axis_index("lon")
    me = lat * LON + lon
    degree = lon * LAT + lat
    core = lax.rem(lon, 2)
    chip = me // 2

    def by_place(d):
        return (d // LON, lax.rem(d, LON))

    def by_degree(d):
        return (lax.rem(d, LAT), d // LAT)

    barrier = pltpu.get_barrier_semaphore()

    def greet(s, carry):
        pl.semaphore_signal(
            barrier, inc=1, device_id=by_place(lax.rem(me + s, NDEV)), device_id_type=MESH
        )
        return carry

    lax.fori_loop(1, NDEV, greet, 0)

    pairs = [
        (x_hbm, x), (saved_hbm, saved), (up_hbm, up), (gout_hbm, gout), (down_hbm, down),
        (fo_hbm, fo), (ta_hbm, ta), (filt_hbm.at[lat], filt), (ts_hbm, ts),
    ]
    loads = [pltpu.make_async_copy(s, d, load_sem.at[i]) for i, (s, d) in enumerate(pairs)]
    for load in loads:
        load.start()

    def scatter(src, dst, n, where, mine, slot):
        def one(s, carry):
            d = lax.rem(mine + s, NDEV)
            pltpu.make_async_remote_copy(
                src_ref=src.at[d],
                dst_ref=dst.at[slot],
                send_sem=ssem.at[n],
                recv_sem=rsem.at[n],
                device_id=where(d),
                device_id_type=MESH,
            ).start()
            return carry

        lax.fori_loop(1, NDEV, one, 0)
        pltpu.make_async_copy(src.at[mine], dst.at[slot], rsem.at[n]).start()

    def arrived(dst, n):
        pltpu.make_async_copy(dst, dst, rsem.at[n]).wait()

    def sent(src, n):
        some = src.at[pl.ds(0, NDEV - 1)]
        pltpu.make_async_copy(some, some, ssem.at[n]).wait()

    lane = lax.broadcasted_iota(jnp.int32, (8, 128), 1)

    def to_channels(values, dst):
        for c in range(3):
            for h in range(2):
                block = values[h * 128 : h * 128 + 128, c * 128 : c * 128 + 128]
                dst[:, c * 2 + h, :] = block.T

    def regroup_in(src):
        for c in range(3):
            for h in range(2):
                for top in range(2):
                    tiles = [
                        src[pl.ds(top * 8 + s, 8, stride=16), c * 2 + h, :] for s in range(8)
                    ]
                    for s, tile in enumerate(exchange(tiles, lane)):
                        circle[top, pl.ds(c * 128 + h * 8 + s, 8, stride=16), :] = tile

    def regroup_out(dst):
        for c in range(3):
            for h in range(2):
                for top in range(2):
                    tiles = [
                        circle[top, pl.ds(c * 128 + h * 8 + s, 8, stride=16), :]
                        for s in range(8)
                    ]
                    for s, tile in enumerate(exchange(tiles, lane)):
                        dst[pl.ds(top * 8 + s, 8, stride=16), c * 2 + h, :] = tile

    def per_order(table):
        def eight(i, carry):
            for u in range(8):
                m = i * 8 + u
                z = zbuf[m]
                high = z.astype(BF16).astype(F32)
                rows = jnp.concatenate([high, z - high], axis=0).astype(BF16)
                r = lax.dot_general(rows, table[m], NN, preferred_element_type=F32)
                wbuf[m] = r[:8, :128] + (r[:8, 128:] + r[8:, :128])
            return carry

        lax.fori_loop(0, MODES // 8, eight, 0)

    def analysis(src, dst):
        regroup_in(src)
        fields = split(jnp.concatenate([circle[0], circle[1]], axis=1))
        for p in range(2):
            rows = (fo[0, p * 128 : p * 128 + 128], fo[1, p * 128 : p * 128 + 128])
            y = dot3(rows, fields, NT)
            for c in range(3):
                zbuf[:, p * 3 + c, :] = y[:, c * 128 : c * 128 + 128]
        per_order(ta)
        for c in range(3):
            for p in range(2):
                dst[:, c * 2 + p, :] = wbuf[:, p * 3 + c, :].T

    zbuf[...] = jnp.zeros_like(zbuf)
    loads[0].wait()
    to_channels(x, send1.at[0])
    pl.semaphore_wait(barrier, NDEV - 1)
    scatter(send1.at[0], recv1.at[0], 0, by_place, me, me)

    loads[1].wait()
    loads[2].wait()
    saved2 = split(saved[...])
    up2 = split(up[...])
    act[...] = dot3(saved2, up2, NN)
    loads[3].wait()
    loads[4].wait()
    gout2 = split(gout[...])
    gpre[...] = dot3(gout2, split(down[...]), NT)
    pre = act[...]
    scale = math.sqrt(2.0 / math.pi)
    square = pre * pre
    t = jnp.tanh(scale * (pre + 0.044715 * (square * pre)))
    half = 0.5 * (1.0 + t)
    act[...] = pre * half
    gpre[...] = gpre[...] * (
        half + (0.5 * scale) * pre * (1.0 - t * t) * (1.0 + (3.0 * 0.044715) * square)
    )
    field[...] = gout[...] + dot3(split(gpre[...]), up2, NT)
    to_channels(field, send1.at[1])
    scatter(send1.at[1], recv1.at[1], 1, by_place, me, me)

    def cut(first):
        for to in range(2):
            for k in range(6):
                for n in range(3):
                    pieces[to, :, n, first + k, :] = part[n, pl.ds(6 * to + k, 64, stride=12), :]

    def share_of(rows, columns, first):
        product = dot3(split(rows[...]), split(columns[...]), TN)
        for n in range(3):
            part[n] = product[:, n * 128 : n * 128 + 128]
        cut(first)

    share_of(gpre, saved, 0)
    share_of(act, gout, 6)
    partner = pltpu.make_async_remote_copy(
        src_ref=pieces.at[1 - core],
        dst_ref=pair,
        send_sem=psem.at[0],
        recv_sem=psem.at[1],
        device_id=(lat, lon + 1 - 2 * core),
        device_id_type=MESH,
    )
    partner.start()

    loads[5].wait()
    loads[6].wait()
    arrived(recv1.at[0], 0)
    analysis(recv1.at[0], send2.at[0])
    scatter(send2.at[0], recv2.at[0], 2, by_degree, degree, me)
    arrived(recv1.at[1], 1)
    analysis(recv1.at[1], send2.at[1])
    scatter(send2.at[1], recv2.at[1], 3, by_degree, degree, me)

    partner.wait()
    for n in range(3):
        for k in range(12):
            pair[:, n, k, :] = pair[:, n, k, :] + pieces[core, :, n, k, :]

    def owner(s, carry):
        d = lax.rem(chip + s, NDEV // 2)
        pltpu.make_async_remote_copy(
            src_ref=pair.at[d],
            dst_ref=others.at[chip],
            send_sem=osem.at[0],
            recv_sem=osem.at[1],
            device_id=by_place(2 * d + core),
            device_id_type=MESH,
        ).start()
        return carry

    lax.fori_loop(1, NDEV // 2, owner, 0)
    pltpu.make_async_copy(pair.at[chip], others.at[chip], osem.at[1]).start()

    loads[7].wait()
    arrived(recv2.at[1], 3)
    for c in range(3):
        for p in range(2):
            spec[1, c * 128 : c * 128 + 128, p * 128 : p * 128 + 128] = recv2[1, :, c * 2 + p, :]
    gspec2 = split(spec[1])
    coef = dot3(split(filt[...]), gspec2, NN)
    for c in range(3):
        for p in range(2):
            send3[:, c * 2 + p, :] = coef[c * 128 : c * 128 + 128, p * 128 : p * 128 + 128]
    scatter(send3, recv3, 4, by_place, me, degree)

    arrived(recv2.at[0], 2)
    for c in range(3):
        for p in range(2):
            spec[0, c * 128 : c * 128 + 128, p * 128 : p * 128 + 128] = recv2[0, :, c * 2 + p, :]
    gfil[...] = dot3(split(spec[0]), split(spec[1]), NT) * (
        1.0 / math.sqrt(2.0 * SAMPLES * MODES)
    )
    share = WIDTH // LAT

    def rows_of(d):
        return gfil.at[pl.ds(pl.multiple_of(d * share, 8), share)]

    def column(s, carry):
        d = lax.rem(lat + s, LAT)
        pltpu.make_async_remote_copy(
            src_ref=rows_of(d),
            dst_ref=gfrecv.at[lat],
            send_sem=gsem.at[0],
            recv_sem=gsem.at[1],
            device_id=(d, lon),
            device_id_type=MESH,
        ).start()
        return carry

    lax.fori_loop(1, LAT, column, 0)
    pltpu.make_async_copy(rows_of(lat), gfrecv.at[lat], gsem.at[1]).start()

    loads[8].wait()
    arrived(recv3, 4)
    for c in range(3):
        for p in range(2):
            zbuf[:, p * 3 + c, :] = recv3[:, c * 2 + p, :].T
    per_order(ts)
    for c in range(3):
        for p in range(2):
            spec[0, c * 128 : c * 128 + 128, p * 128 : p * 128 + 128] = wbuf[:, p * 3 + c, :].T
    grid = dot3(split(spec[0]), (fo[0], fo[1]), NN)
    circle[0] = grid[:, :128]
    circle[1] = grid[:, 128:]
    regroup_out(send4)
    scatter(send4, recv4, 5, by_place, me, me)

    pltpu.make_async_copy(others, others, osem.at[1]).wait()
    point_scale = 1.0 / math.sqrt(SAMPLES * NLAT * NLON)
    sums[...] = jnp.sum(others[...], axis=0) * point_scale
    pltpu.make_async_copy(gfrecv, gfrecv, gsem.at[1]).wait()
    stores = [
        pltpu.make_async_copy(sums, up_out, out_sem.at[0]),
        pltpu.make_async_copy(gfrecv, gf_out, out_sem.at[1]),
    ]
    for store in stores:
        store.start()

    arrived(recv4, 5)
    for c in range(3):
        for h in range(2):
            rows, lanes = slice(h * 128, h * 128 + 128), slice(c * 128, c * 128 + 128)
            field[rows, lanes] = field[rows, lanes] + recv4[:, c * 2 + h, :].T
    last = pltpu.make_async_copy(field, gin_out, out_sem.at[2])
    last.start()

    sent(send1.at[0], 0)
    sent(send1.at[1], 1)
    sent(send2.at[0], 2)
    sent(send2.at[1], 3)
    sent(send3, 4)
    sent(send4, 5)
    some = pair.at[pl.ds(0, NDEV // 2 - 1)]
    pltpu.make_async_copy(some, some, osem.at[0]).wait()
    some = gfil.at[pl.ds(0, WIDTH - share)]
    pltpu.make_async_copy(some, some, gsem.at[0]).wait()
    for store in stores:
        store.wait()
    last.wait()


def shards(inputs, saved, grad_out, w_up, w_down, w_filter):
    legendre = legendre_values()
    ta = np.concatenate(halves(legendre.transpose(0, 2, 1)), axis=2)
    ts = np.concatenate(halves(legendre), axis=2)
    fo = np.stack(halves(fourier_values().T))
    anywhere = pl.BlockSpec(memory_space=pl.ANY)

    def block():
        return pltpu.VMEM((NDEV, 6, 128), F32)

    def blocks(n):
        return pltpu.VMEM((n, NDEV, 6, 128), F32)

    gin, sums, gfil = pl.pallas_call(
        kernel,
        out_shape=(
            jax.ShapeDtypeStruct((POINTS, WIDTH), F32),
            jax.ShapeDtypeStruct((3, 12, 128), F32),
            jax.ShapeDtypeStruct((LAT, WIDTH // LAT, WIDTH), F32),
        ),
        in_specs=[anywhere] * 9,
        out_specs=(anywhere,) * 3,
        scratch_shapes=[
            pltpu.VMEM((POINTS, WIDTH), F32),
            pltpu.VMEM((POINTS, WIDTH), F32),
            pltpu.VMEM((POINTS, WIDTH), F32),
            pltpu.VMEM((WIDTH, HIDDEN), F32),
            pltpu.VMEM((HIDDEN, WIDTH), F32),
            pltpu.VMEM((WIDTH, WIDTH), F32),
            pltpu.VMEM((MODES, NLAT, 256), BF16),
            pltpu.VMEM((MODES, MODES, 256), BF16),
            pltpu.VMEM((2, 256, 256), BF16),
            blocks(2), blocks(2), blocks(2), blocks(2), block(), block(), block(), block(),
            pltpu.VMEM((POINTS, HIDDEN), F32),
            pltpu.VMEM((POINTS, HIDDEN), F32),
            pltpu.VMEM((POINTS, WIDTH), F32),
            pltpu.VMEM((3, HIDDEN, 128), F32),
            pltpu.VMEM((2, NDEV // 2, 3, 12, 128), F32),
            pltpu.VMEM((NDEV // 2, 3, 12, 128), F32),
            pltpu.VMEM((NDEV // 2, 3, 12, 128), F32),
            pltpu.VMEM((2, WIDTH, 128), F32),
            pltpu.VMEM((MODES, 8, 128), F32),
            pltpu.VMEM((MODES, 8, 128), F32),
            pltpu.VMEM((2, WIDTH, 256), F32),
            pltpu.VMEM((WIDTH, WIDTH), F32),
            pltpu.VMEM((LAT, WIDTH // LAT, WIDTH), F32),
            pltpu.VMEM((3, 12, 128), F32),
            pltpu.SemaphoreType.DMA((9,)),
            pltpu.SemaphoreType.DMA((6,)),
            pltpu.SemaphoreType.DMA((6,)),
            pltpu.SemaphoreType.DMA((2,)),
            pltpu.SemaphoreType.DMA((2,)),
            pltpu.SemaphoreType.DMA((2,)),
            pltpu.SemaphoreType.DMA((3,)),
        ],
        compiler_params=pltpu.CompilerParams(
            collective_id=0, has_side_effects=True, vmem_limit_bytes=56 << 20
        ),
    )(
        inputs.reshape(POINTS, WIDTH), saved.reshape(POINTS, WIDTH),
        grad_out.reshape(POINTS, WIDTH), w_up, w_down, w_filter,
        jnp.asarray(ta), jnp.asarray(ts), jnp.asarray(fo),
    )
    sums = sums.transpose(1, 0, 2).reshape(12, WIDTH)
    return (gin.reshape(inputs.shape), sums[:6].T, sums[6:], gfil)


def solution(mesh):
    in_specs = (
        P(None, "lat", "lon", None),
        P(None, "lat", "lon", None),
        P(None, "lat", "lon", None),
        P(),
        P(),
        P("lon", None, None),
    )
    out_specs = (
        P(None, "lat", "lon", None),
        P(None, ("lat", "lon")),
        P(("lat", "lon"), None),
        P("lon", "lat", None),
    )
    return jax.shard_map(shards, mesh=mesh, in_specs=in_specs, out_specs=out_specs, check_vma=False)
```

profile of v0, /device:TPU:1, one launch (start us, length us, event | category | flops | bytes accessed | tf_op | source)
XLA Modules:
  0.0 85.2 jit_solution(6377230813078871895)
XLA Ops:
  0.6 79.4 %shard_map.120 = (f32[256,384]{1,0:T(8,128)}, f32[3,12,128]{2,1,0:T(8,128)}, f32[8,48,384]{2,1,0:T(8,128)}) custom-call(f32[256,384]{1,0:T(8,128)} %bitcast.12, f32[256,384]{1,0:T(8,128)} %bitcast.13, f32[256,384]{1,0:T(8,128)} %bitcast.14, f32[384,768]{1,0:T(8,128)} %up_hbm.1, f32[768,384]{1,0:T(8,128)} %down_hbm.1, f32[8,384,384]{2,1,0:T(8,128)} %filt_hbm.1, ...), custom_call_target="tpu_custom_call" | custom-call | tf_op jit(solution)/shard_map/pallas_call | solution.py:395
  80.1 1.4 %slice_bitcast_fusion = (f32[6,384]{1,0:T(8,128)}, f32[384,6]{0,1:T(8,128)}) fusion(f32[12,3,128]{2,0,1:T(8,128)} %bitcast.15), kind=kLoop, calls=%fused_computation | loop fusion | bytes 36864 | tf_op jit(solution)/shard_map/slice | solution.py:446
  81.5 1.8 %copy.15 = f32[1,16,16,384]{3,2,1,0:T(8,128)} copy(f32[1,16,16,384]{3,2,1,0:T(8,128)} %bitcast.11) | data formatting | bytes 786432
  83.2 1.9 %copy.16 = f32[8,48,384]{2,1,0:T(8,128)} copy(f32[8,48,384]{2,1,0:T(8,128)} %get-tuple-element.19) | data formatting | bytes 1179648
where the time goes:
time: 85.4 us; the launch traced here: 85.2 us
  Pallas kernels  79.4 us (93%)
  local copies, waits for them, and re-layouts  5.08 us (6%)
    pallas_call x1, Pallas kernels, shards(): pl.pallas_call(kernel, out_shape=(jax.ShapeDtypeStruct((POINTS, WIDTH), F...  79.4 us
    unnamed x2, local copies, waits for them, and re-layouts  3.68 us

commit v1 on v0

--- a/solution.py
+++ b/solution.py
@@ -18,6 +18,12 @@
 LON = 16
 LAT = 8
 POINTS = 256
+EARLY = 2
+AWAY = (0, 1, 2, 1)
+STEPS = sorted(
+    [(i // 32, i // 8 % 4, i // 2 % 4, i % 2) for i in range(1, NDEV)],
+    key=lambda step: -sum(AWAY[k] for k in step[:3]),
+)
 MESH = pl.DeviceIdType.MESH
 F32 = jnp.float32
 BF16 = jnp.bfloat16
@@ -104,15 +110,24 @@
     lat = lax.axis_index("lat")
     lon = lax.axis_index("lon")
     me = lat * LON + lon
-    degree = lon * LAT + lat
     core = lax.rem(lon, 2)
     chip = me // 2
 
     def by_place(d):
         return (d // LON, lax.rem(d, LON))
 
-    def by_degree(d):
-        return (lax.rem(d, LAT), d // LAT)
+    x_at, y_lo = lax.rem(lat, 4), lat // 4
+    z_at, y_hi = lax.rem(lon // 2, 4), lon // 8
+    y_at = y_hi * 2 + y_lo
+    ys = [lax.rem(y_at + i, 4) for i in range(4)]
+    lats = [[lax.rem(y, 2) * 4 + lax.rem(x_at + i, 4) for i in range(4)] for y in ys]
+    lons = [
+        [
+            [(y // 2) * 8 + lax.rem(z_at + i, 4) * 2 + lax.rem(core + c, 2) for c in range(2)]
+            for i in range(4)
+        ]
+        for y in ys
+    ]
 
     barrier = pltpu.get_barrier_semaphore()
 
@@ -125,28 +140,26 @@
     lax.fori_loop(1, NDEV, greet, 0)
 
     pairs = [
-        (x_hbm, x), (saved_hbm, saved), (up_hbm, up), (gout_hbm, gout), (down_hbm, down),
+        (saved_hbm, saved), (up_hbm, up), (gout_hbm, gout), (down_hbm, down), (x_hbm, x),
         (fo_hbm, fo), (ta_hbm, ta), (filt_hbm.at[lat], filt), (ts_hbm, ts),
     ]
     loads = [pltpu.make_async_copy(s, d, load_sem.at[i]) for i, (s, d) in enumerate(pairs)]
     for load in loads:
         load.start()
 
-    def scatter(src, dst, n, where, mine, slot):
-        def one(s, carry):
-            d = lax.rem(mine + s, NDEV)
+    def scatter(src, dst, n):
+        for y, x_, z, c in STEPS:
+            to_lat = lats[y][x_]
+            to_lon = lons[y][z][c]
             pltpu.make_async_remote_copy(
-                src_ref=src.at[d],
-                dst_ref=dst.at[slot],
+                src_ref=src.at[to_lat * LON + to_lon],
+                dst_ref=dst.at[me],
                 send_sem=ssem.at[n],
                 recv_sem=rsem.at[n],
-                device_id=where(d),
+                device_id=(to_lat, to_lon),
                 device_id_type=MESH,
             ).start()
-            return carry
-
-        lax.fori_loop(1, NDEV, one, 0)
-        pltpu.make_async_copy(src.at[mine], dst.at[slot], rsem.at[n]).start()
+        pltpu.make_async_copy(src.at[me], dst.at[me], rsem.at[n]).start()
 
     def arrived(dst, n):
         pltpu.make_async_copy(dst, dst, rsem.at[n]).wait()
@@ -210,19 +223,13 @@
             for p in range(2):
                 dst[:, c * 2 + p, :] = wbuf[:, p * 3 + c, :].T
 
-    zbuf[...] = jnp.zeros_like(zbuf)
     loads[0].wait()
-    to_channels(x, send1.at[0])
-    pl.semaphore_wait(barrier, NDEV - 1)
-    scatter(send1.at[0], recv1.at[0], 0, by_place, me, me)
-
     loads[1].wait()
-    loads[2].wait()
     saved2 = split(saved[...])
     up2 = split(up[...])
     act[...] = dot3(saved2, up2, NN)
+    loads[2].wait()
     loads[3].wait()
-    loads[4].wait()
     gout2 = split(gout[...])
     gpre[...] = dot3(gout2, split(down[...]), NT)
     pre = act[...]
@@ -236,7 +243,13 @@
     )
     field[...] = gout[...] + dot3(split(gpre[...]), up2, NT)
     to_channels(field, send1.at[1])
-    scatter(send1.at[1], recv1.at[1], 1, by_place, me, me)
+    pl.semaphore_wait(barrier, NDEV - 1)
+    scatter(send1.at[1], recv1.at[1], 1)
+
+    loads[4].wait()
+    to_channels(x, send1.at[0])
+    scatter(send1.at[0], recv1.at[0], 0)
+    zbuf[...] = jnp.zeros_like(zbuf)
 
     def cut(first):
         for to in range(2):
@@ -264,17 +277,12 @@
 
     loads[5].wait()
     loads[6].wait()
-    arrived(recv1.at[0], 0)
-    analysis(recv1.at[0], send2.at[0])
-    scatter(send2.at[0], recv2.at[0], 2, by_degree, degree, me)
     arrived(recv1.at[1], 1)
     analysis(recv1.at[1], send2.at[1])
-    scatter(send2.at[1], recv2.at[1], 3, by_degree, degree, me)
+    scatter(send2.at[1], recv2.at[1], 3)
 
     partner.wait()
-    for n in range(3):
-        for k in range(12):
-            pair[:, n, k, :] = pair[:, n, k, :] + pieces[core, :, n, k, :]
+    pair[...] = pair[...] + pieces[core]
 
     def owner(s, carry):
         d = lax.rem(chip + s, NDEV // 2)
@@ -288,8 +296,12 @@
         ).start()
         return carry
 
-    lax.fori_loop(1, NDEV // 2, owner, 0)
+    lax.fori_loop(1, EARLY, owner, 0)
     pltpu.make_async_copy(pair.at[chip], others.at[chip], osem.at[1]).start()
+
+    arrived(recv1.at[0], 0)
+    analysis(recv1.at[0], send2.at[0])
+    scatter(send2.at[0], recv2.at[0], 2)
 
     loads[7].wait()
     arrived(recv2.at[1], 3)
@@ -301,7 +313,7 @@
     for c in range(3):
         for p in range(2):
             send3[:, c * 2 + p, :] = coef[c * 128 : c * 128 + 128, p * 128 : p * 128 + 128]
-    scatter(send3, recv3, 4, by_place, me, degree)
+    scatter(send3, recv3, 4)
 
     arrived(recv2.at[0], 2)
     for c in range(3):
@@ -329,6 +341,7 @@
 
     lax.fori_loop(1, LAT, column, 0)
     pltpu.make_async_copy(rows_of(lat), gfrecv.at[lat], gsem.at[1]).start()
+    lax.fori_loop(EARLY, NDEV // 2, owner, 0)
 
     loads[8].wait()
     arrived(recv3, 4)
@@ -343,11 +356,14 @@
     circle[0] = grid[:, :128]
     circle[1] = grid[:, 128:]
     regroup_out(send4)
-    scatter(send4, recv4, 5, by_place, me, me)
+    scatter(send4, recv4, 5)
 
     pltpu.make_async_copy(others, others, osem.at[1]).wait()
     point_scale = 1.0 / math.sqrt(SAMPLES * NLAT * NLON)
-    sums[...] = jnp.sum(others[...], axis=0) * point_scale
+    total = jnp.sum(others[...], axis=0) * point_scale
+    for n in range(3):
+        sums[0, :, n * 128 : n * 128 + 128] = total[n, :6]
+        sums[1, :, n * 128 : n * 128 + 128] = total[n, 6:]
     pltpu.make_async_copy(gfrecv, gfrecv, gsem.at[1]).wait()
     stores = [
         pltpu.make_async_copy(sums, up_out, out_sem.at[0]),
@@ -379,8 +395,28 @@
     last.wait()
 
 
+def results(gin, sums, gfil, gin_out, up_out, down_out, gfil_out, a, b, c, sem, out_sem):
+    loads = [
+        pltpu.make_async_copy(gfil, c, sem.at[0]),
+        pltpu.make_async_copy(gin, a, sem.at[1]),
+        pltpu.make_async_copy(sums, b, sem.at[2]),
+    ]
+    pairs = [(c, gfil_out), (a, gin_out), (b.at[0], up_out), (b.at[1], down_out)]
+    stores = [pltpu.make_async_copy(s, d, out_sem.at[i]) for i, (s, d) in enumerate(pairs)]
+    for load in loads:
+        load.start()
+    for i, store in enumerate(stores):
+        if i < 3:
+            loads[i].wait()
+        store.start()
+    for store in stores:
+        store.wait()
+
+
 def shards(inputs, saved, grad_out, w_up, w_down, w_filter):
     legendre = legendre_values()
+    device = np.arange(NDEV)
+    legendre = legendre[:, (device % LON) * LAT + device // LON]
     ta = np.concatenate(halves(legendre.transpose(0, 2, 1)), axis=2)
     ts = np.concatenate(halves(legendre), axis=2)
     fo = np.stack(halves(fourier_values().T))
@@ -396,7 +432,7 @@
         kernel,
         out_shape=(
             jax.ShapeDtypeStruct((POINTS, WIDTH), F32),
-            jax.ShapeDtypeStruct((3, 12, 128), F32),
+            jax.ShapeDtypeStruct((2, 6, WIDTH), F32),
             jax.ShapeDtypeStruct((LAT, WIDTH // LAT, WIDTH), F32),
         ),
         in_specs=[anywhere] * 9,
@@ -425,7 +461,7 @@
             pltpu.VMEM((2, WIDTH, 256), F32),
             pltpu.VMEM((WIDTH, WIDTH), F32),
             pltpu.VMEM((LAT, WIDTH // LAT, WIDTH), F32),
-            pltpu.VMEM((3, 12, 128), F32),
+            pltpu.VMEM((2, 6, WIDTH), F32),
             pltpu.SemaphoreType.DMA((9,)),
             pltpu.SemaphoreType.DMA((6,)),
             pltpu.SemaphoreType.DMA((6,)),
@@ -442,8 +478,25 @@
         grad_out.reshape(POINTS, WIDTH), w_up, w_down, w_filter,
         jnp.asarray(ta), jnp.asarray(ts), jnp.asarray(fo),
     )
-    sums = sums.transpose(1, 0, 2).reshape(12, WIDTH)
-    return (gin.reshape(inputs.shape), sums[:6].T, sums[6:], gfil)
+    gin, up, down, gfil = pl.pallas_call(
+        results,
+        out_shape=(
+            jax.ShapeDtypeStruct((POINTS, WIDTH), F32),
+            jax.ShapeDtypeStruct((6, WIDTH), F32),
+            jax.ShapeDtypeStruct((6, WIDTH), F32),
+            jax.ShapeDtypeStruct((LAT, WIDTH // LAT, WIDTH), F32),
+        ),
+        in_specs=[anywhere] * 3,
+        out_specs=(anywhere,) * 4,
+        scratch_shapes=[
+            pltpu.VMEM((POINTS, WIDTH), F32),
+            pltpu.VMEM((2, 6, WIDTH), F32),
+            pltpu.VMEM((LAT, WIDTH // LAT, WIDTH), F32),
+            pltpu.SemaphoreType.DMA((3,)),
+            pltpu.SemaphoreType.DMA((4,)),
+        ],
+    )(gin, sums, gfil)
+    return (gin.reshape(inputs.shape), up.T, down, gfil)
 
 
 def solution(mesh):

time: 85.4 us -> 74.2 us (0.87)
  Pallas kernels: 79.4 us -> 73.2 us
  local copies, waits for them, and re-layouts: 5.08 us -> 0 us
    pallas_call x1, Pallas kernels: 79.4 us -> 71.2 us  [shards(): pl.pallas_call(kernel, out_shape=(jax.ShapeDtypeStruct((POINTS, WIDTH), F...]
    unnamed x2 -> x0, local copies, waits for them, and re-layouts: 3.68 us -> none
    pallas_call x0 -> x1, Pallas kernels: none -> 2.07 us  [shards(): pl.pallas_call(results, out_shape=(jax.ShapeDtypeStruct((POINTS, WIDTH),...]
    slice x1 -> x0, local copies, waits for them, and re-layouts: 1.39 us -> none  [shards(): return (gin.reshape(inputs.shape), sums[:6].T, sums[6:], gfil)]
where the time goes in v1:
time: 74.2 us; the launch traced here: 74 us
  Pallas kernels  73.2 us (99%)
  between operations  0.8 us (1%)
    pallas_call x1, Pallas kernels, shards(): pl.pallas_call(kernel, out_shape=(jax.ShapeDtypeStruct((POINTS, WIDTH), F...  71.2 us
    pallas_call x1, Pallas kernels, shards(): pl.pallas_call(results, out_shape=(jax.ShapeDtypeStruct((POINTS, WIDTH),...  2.07 us

profile of v1, /device:TPU:1, one launch (start us, length us, event | category | flops | bytes accessed | tf_op | source)
XLA Modules:
  0.0 74.0 jit_solution(5096832841818375645)
XLA Ops:
  0.6 71.2 %shard_map.120 = (f32[256,384]{1,0:T(8,128)}, f32[2,6,384]{2,1,0:T(8,128)}, f32[8,48,384]{2,1,0:T(8,128)}) custom-call(f32[256,384]{1,0:T(8,128)} %bitcast.5, f32[256,384]{1,0:T(8,128)} %bitcast.6, f32[256,384]{1,0:T(8,128)} %bitcast.7, f32[384,768]{1,0:T(8,128)} %up_hbm.1, f32[768,384]{1,0:T(8,128)} %down_hbm.1, f32[8,384,384]{2,1,0:T(8,128)} %filt_hbm.1, ...), custom_call_target="tpu_custom_call" | custom-call | tf_op jit(solution)/shard_map/pallas_call | solution.py:431
  71.8 2.1 %shard_map.121 = (f32[256,384]{1,0:T(8,128)}, f32[6,384]{1,0:T(8,128)}, f32[6,384]{1,0:T(8,128)}, f32[8,48,384]{2,1,0:T(8,128)}) custom-call(f32[256,384]{1,0:T(8,128)} %get-tuple-element.11.gin, f32[2,6,384]{2,1,0:T(8,128)} %get-tuple-element.12.sums, f32[8,48,384]{2,1,0:T(8,128)} %get-tuple-element.13.gfil), custom_call_target="tpu_custom_call" | custom-call | tf_op jit(solution)/shard_map/pallas_call | solution.py:481

commit v2 on v1

--- a/solution.py
+++ b/solution.py
@@ -18,7 +18,7 @@
 LON = 16
 LAT = 8
 POINTS = 256
-EARLY = 2
+BLOCK = 32
 AWAY = (0, 1, 2, 1)
 STEPS = sorted(
     [(i // 32, i // 8 % 4, i // 2 % 4, i % 2) for i in range(1, NDEV)],
@@ -104,14 +104,13 @@
     gin_out, up_out, gf_out,
     x, saved, gout, up, down, filt, ta, ts, fo,
     send1, recv1, send2, recv2, send3, recv3, send4, recv4,
-    act, gpre, field, part, pieces, pair, others, circle, zbuf, wbuf, spec, gfil, gfrecv, sums,
+    act, gpre, field, part, pieces, pair, ring, mid, others, circle, zbuf, wbuf, spec, gfil, gfrecv, sums,
     load_sem, ssem, rsem, psem, osem, gsem, out_sem,
 ):
     lat = lax.axis_index("lat")
     lon = lax.axis_index("lon")
     me = lat * LON + lon
     core = lax.rem(lon, 2)
-    chip = me // 2
 
     def by_place(d):
         return (d // LON, lax.rem(d, LON))
@@ -198,9 +197,9 @@
                         dst[pl.ds(top * 8 + s, 8, stride=16), c * 2 + h, :] = tile
 
     def per_order(table):
-        def eight(i, carry):
-            for u in range(8):
-                m = i * 8 + u
+        def several(i, carry):
+            for u in range(BLOCK):
+                m = i * BLOCK + u
                 z = zbuf[m]
                 high = z.astype(BF16).astype(F32)
                 rows = jnp.concatenate([high, z - high], axis=0).astype(BF16)
@@ -208,7 +207,7 @@
                 wbuf[m] = r[:8, :128] + (r[:8, 128:] + r[8:, :128])
             return carry
 
-        lax.fori_loop(0, MODES // 8, eight, 0)
+        lax.fori_loop(0, MODES // BLOCK, several, 0)
 
     def analysis(src, dst):
         regroup_in(src)
@@ -254,8 +253,17 @@
     def cut(first):
         for to in range(2):
             for k in range(6):
-                for n in range(3):
-                    pieces[to, :, n, first + k, :] = part[n, pl.ds(6 * to + k, 64, stride=12), :]
+
+                def put(n, at, chip, count, step, to=to, k=k):
+                    rows = pl.ds(6 * to + k + 12 * chip, count, stride=12 * step)
+                    pieces[to, n, at : at + count, first + k, :] = part[n, rows, :]
+
+                for i in range(4):
+                    for low in range(2):
+                        put(0, i * 16 + low * 8, low * 32 + i * 8, 8, 1)
+                    for j in range(4):
+                        put(1, i * 16 + j * 4, i % 2 * 32 + j * 8 + i // 2 * 4, 4, 1)
+                    put(2, i * 16, i, 16, 4)
 
     def share_of(rows, columns, first):
         product = dot3(split(rows[...]), split(columns[...]), TN)
@@ -283,21 +291,27 @@
 
     partner.wait()
     pair[...] = pair[...] + pieces[core]
-
-    def owner(s, carry):
-        d = lax.rem(chip + s, NDEV // 2)
-        pltpu.make_async_remote_copy(
-            src_ref=pair.at[d],
-            dst_ref=others.at[chip],
-            send_sem=osem.at[0],
-            recv_sem=osem.at[1],
-            device_id=by_place(2 * d + core),
-            device_id_type=MESH,
-        ).start()
-        return carry
-
-    lax.fori_loop(1, EARLY, owner, 0)
-    pltpu.make_async_copy(pair.at[chip], others.at[chip], osem.at[1]).start()
+    places = (x_at, y_at, z_at)
+
+    def beside(n, step):
+        if n == 0:
+            return (y_lo * 4 + lax.rem(x_at + step, 4), lon)
+        if n == 1:
+            y = lax.rem(y_at + step, 4)
+            return (lax.rem(y, 2) * 4 + x_at, (y // 2) * 8 + z_at * 2 + core)
+        return (lat, y_hi * 8 + lax.rem(z_at + step, 4) * 2 + core)
+
+    for step in (2, 1, 3):
+        for n in range(3):
+            to = lax.rem(places[n] + step, 4)
+            pltpu.make_async_remote_copy(
+                src_ref=pair.at[n, pl.ds(to * 16, 16)],
+                dst_ref=ring.at[n, step - 1],
+                send_sem=psem.at[2],
+                recv_sem=psem.at[3],
+                device_id=beside(n, step),
+                device_id_type=MESH,
+            ).start()
 
     arrived(recv1.at[0], 0)
     analysis(recv1.at[0], send2.at[0])
@@ -315,6 +329,36 @@
             send3[:, c * 2 + p, :] = coef[c * 128 : c * 128 + 128, p * 128 : p * 128 + 128]
     scatter(send3, recv3, 4)
 
+    pltpu.make_async_copy(ring, ring, psem.at[3]).wait()
+    for n in range(3):
+        own = pair[n, pl.ds(places[n] * 16, 16)]
+        mid[n] = (own + ring[n, 0]) + (ring[n, 1] + ring[n, 2])
+    planes = (y_lo * 8 + y_hi * 4 + z_at, x_at * 4 + z_at, y_lo * 8 + x_at * 2 + y_hi)
+
+    def across(n, p):
+        if n == 0:
+            return ((p // 8) * 4 + x_at, lax.rem(p // 4, 2) * 8 + lax.rem(p, 4) * 2 + core)
+        if n == 1:
+            return (y_lo * 4 + p // 4, y_hi * 8 + lax.rem(p, 4) * 2 + core)
+        return ((p // 8) * 4 + lax.rem(p // 2, 4), lax.rem(p, 2) * 8 + z_at * 2 + core)
+
+    def spread(s, carry):
+        for n in range(3):
+            p = lax.rem(planes[n] + s, 16)
+            pltpu.make_async_remote_copy(
+                src_ref=mid.at[n, p],
+                dst_ref=others.at[n, planes[n]],
+                send_sem=osem.at[0],
+                recv_sem=osem.at[1],
+                device_id=across(n, p),
+                device_id_type=MESH,
+            ).start()
+        return carry
+
+    lax.fori_loop(1, 16, spread, 0)
+    for n in range(3):
+        pltpu.make_async_copy(mid.at[n, planes[n]], others.at[n, planes[n]], osem.at[1]).start()
+
     arrived(recv2.at[0], 2)
     for c in range(3):
         for p in range(2):
@@ -341,8 +385,6 @@
 
     lax.fori_loop(1, LAT, column, 0)
     pltpu.make_async_copy(rows_of(lat), gfrecv.at[lat], gsem.at[1]).start()
-    lax.fori_loop(EARLY, NDEV // 2, owner, 0)
-
     loads[8].wait()
     arrived(recv3, 4)
     for c in range(3):
@@ -360,10 +402,10 @@
 
     pltpu.make_async_copy(others, others, osem.at[1]).wait()
     point_scale = 1.0 / math.sqrt(SAMPLES * NLAT * NLON)
-    total = jnp.sum(others[...], axis=0) * point_scale
     for n in range(3):
-        sums[0, :, n * 128 : n * 128 + 128] = total[n, :6]
-        sums[1, :, n * 128 : n * 128 + 128] = total[n, 6:]
+        total = jnp.sum(others[n], axis=0) * point_scale
+        sums[0, :, n * 128 : n * 128 + 128] = total[:6]
+        sums[1, :, n * 128 : n * 128 + 128] = total[6:]
     pltpu.make_async_copy(gfrecv, gfrecv, gsem.at[1]).wait()
     stores = [
         pltpu.make_async_copy(sums, up_out, out_sem.at[0]),
@@ -386,7 +428,8 @@
     sent(send2.at[1], 3)
     sent(send3, 4)
     sent(send4, 5)
-    some = pair.at[pl.ds(0, NDEV // 2 - 1)]
+    pltpu.make_async_copy(ring, ring, psem.at[2]).wait()
+    some = others.at[:, pl.ds(0, 15)]
     pltpu.make_async_copy(some, some, osem.at[0]).wait()
     some = gfil.at[pl.ds(0, WIDTH - share)]
     pltpu.make_async_copy(some, some, gsem.at[0]).wait()
@@ -452,9 +495,11 @@
             pltpu.VMEM((POINTS, HIDDEN), F32),
             pltpu.VMEM((POINTS, WIDTH), F32),
             pltpu.VMEM((3, HIDDEN, 128), F32),
-            pltpu.VMEM((2, NDEV // 2, 3, 12, 128), F32),
-            pltpu.VMEM((NDEV // 2, 3, 12, 128), F32),
-            pltpu.VMEM((NDEV // 2, 3, 12, 128), F32),
+            pltpu.VMEM((2, 3, NDEV // 2, 12, 128), F32),
+            pltpu.VMEM((3, NDEV // 2, 12, 128), F32),
+            pltpu.VMEM((3, 3, 16, 12, 128), F32),
+            pltpu.VMEM((3, 16, 12, 128), F32),
+            pltpu.VMEM((3, 16, 12, 128), F32),
             pltpu.VMEM((2, WIDTH, 128), F32),
             pltpu.VMEM((MODES, 8, 128), F32),
             pltpu.VMEM((MODES, 8, 128), F32),
@@ -465,7 +510,7 @@
             pltpu.SemaphoreType.DMA((9,)),
             pltpu.SemaphoreType.DMA((6,)),
             pltpu.SemaphoreType.DMA((6,)),
-            pltpu.SemaphoreType.DMA((2,)),
+            pltpu.SemaphoreType.DMA((4,)),
             pltpu.SemaphoreType.DMA((2,)),
             pltpu.SemaphoreType.DMA((2,)),
             pltpu.SemaphoreType.DMA((3,)),

time: 74.2 us -> 65.2 us (0.88)
  Pallas kernels: 73.2 us -> 64.3 us
    pallas_call x1, Pallas kernels: 71.2 us -> 62.2 us  [shards(): pl.pallas_call(kernel, out_shape=(jax.ShapeDtypeStruct((POINTS, WIDTH), F...]
where the time goes in v2:
time: 65.2 us; the launch traced here: 65.1 us
  Pallas kernels  64.3 us (99%)
  between operations  0.8 us (1%)
    pallas_call x1, Pallas kernels, shards(): pl.pallas_call(kernel, out_shape=(jax.ShapeDtypeStruct((POINTS, WIDTH), F...  62.2 us
    pallas_call x1, Pallas kernels, shards(): pl.pallas_call(results, out_shape=(jax.ShapeDtypeStruct((POINTS, WIDTH),...  2.07 us

profile of v2, /device:TPU:1, one launch (start us, length us, event | category | flops | bytes accessed | tf_op | source)
XLA Modules:
  0.0 65.1 jit_solution(18319695170546786570)
XLA Ops:
  0.6 62.2 %shard_map.120 = (f32[256,384]{1,0:T(8,128)}, f32[2,6,384]{2,1,0:T(8,128)}, f32[8,48,384]{2,1,0:T(8,128)}) custom-call(f32[256,384]{1,0:T(8,128)} %bitcast.5, f32[256,384]{1,0:T(8,128)} %bitcast.6, f32[256,384]{1,0:T(8,128)} %bitcast.7, f32[384,768]{1,0:T(8,128)} %up_hbm.1, f32[768,384]{1,0:T(8,128)} %down_hbm.1, f32[8,384,384]{2,1,0:T(8,128)} %filt_hbm.1, ...), custom_call_target="tpu_custom_call" | custom-call | tf_op jit(solution)/shard_map/pallas_call | solution.py:474
  62.8 2.1 %shard_map.121 = (f32[256,384]{1,0:T(8,128)}, f32[6,384]{1,0:T(8,128)}, f32[6,384]{1,0:T(8,128)}, f32[8,48,384]{2,1,0:T(8,128)}) custom-call(f32[256,384]{1,0:T(8,128)} %get-tuple-element.11.gin, f32[2,6,384]{2,1,0:T(8,128)} %get-tuple-element.12.sums, f32[8,48,384]{2,1,0:T(8,128)} %get-tuple-element.13.gfil), custom_call_target="tpu_custom_call" | custom-call | tf_op jit(solution)/shard_map/pallas_call | solution.py:526

commit v3 on v2

--- a/solution.py
+++ b/solution.py
@@ -18,7 +18,7 @@
 LON = 16
 LAT = 8
 POINTS = 256
-BLOCK = 32
+BLOCK = 64
 AWAY = (0, 1, 2, 1)
 STEPS = sorted(
     [(i // 32, i // 8 % 4, i // 2 % 4, i % 2) for i in range(1, NDEV)],
@@ -318,12 +318,13 @@
     scatter(send2.at[0], recv2.at[0], 2)
 
     loads[7].wait()
+    filt2 = split(filt[...])
     arrived(recv2.at[1], 3)
     for c in range(3):
         for p in range(2):
             spec[1, c * 128 : c * 128 + 128, p * 128 : p * 128 + 128] = recv2[1, :, c * 2 + p, :]
     gspec2 = split(spec[1])
-    coef = dot3(split(filt[...]), gspec2, NN)
+    coef = dot3(filt2, gspec2, NN)
     for c in range(3):
         for p in range(2):
             send3[:, c * 2 + p, :] = coef[c * 128 : c * 128 + 128, p * 128 : p * 128 + 128]

time: 65.2 us -> 65 us (level)
  no operation moved by 1% of the time
where the time goes in v3:
time: 65 us; the launch traced here: 64.8 us
  Pallas kernels  64 us (98%)
  between operations  0.8 us (1%)
    pallas_call x1, Pallas kernels, shards(): pl.pallas_call(kernel, out_shape=(jax.ShapeDtypeStruct((POINTS, WIDTH), F...  62 us
    pallas_call x1, Pallas kernels, shards(): pl.pallas_call(results, out_shape=(jax.ShapeDtypeStruct((POINTS, WIDTH),...  2.07 us

profile of v3, /device:TPU:1, one launch (start us, length us, event | category | flops | bytes accessed | tf_op | source)
XLA Modules:
  0.0 64.8 jit_solution(14741740837465173337)
XLA Ops:
  0.6 62.0 %shard_map.120 = (f32[256,384]{1,0:T(8,128)}, f32[2,6,384]{2,1,0:T(8,128)}, f32[8,48,384]{2,1,0:T(8,128)}) custom-call(f32[256,384]{1,0:T(8,128)} %bitcast.5, f32[256,384]{1,0:T(8,128)} %bitcast.6, f32[256,384]{1,0:T(8,128)} %bitcast.7, f32[384,768]{1,0:T(8,128)} %up_hbm.1, f32[768,384]{1,0:T(8,128)} %down_hbm.1, f32[8,384,384]{2,1,0:T(8,128)} %filt_hbm.1, ...), custom_call_target="tpu_custom_call" | custom-call | tf_op jit(solution)/shard_map/pallas_call | solution.py:475
  62.6 2.1 %shard_map.121 = (f32[256,384]{1,0:T(8,128)}, f32[6,384]{1,0:T(8,128)}, f32[6,384]{1,0:T(8,128)}, f32[8,48,384]{2,1,0:T(8,128)}) custom-call(f32[256,384]{1,0:T(8,128)} %get-tuple-element.11.gin, f32[2,6,384]{2,1,0:T(8,128)} %get-tuple-element.12.sums, f32[8,48,384]{2,1,0:T(8,128)} %get-tuple-element.13.gfil), custom_call_target="tpu_custom_call" | custom-call | tf_op jit(solution)/shard_map/pallas_call | solution.py:527
